TPU v7x, 32 devices: a whole 2x2x4 slice. The times are simulated.
32 devices in a mesh: row: 4 (over y, x), col: 8 (over z, core).
Axes of the slice: x: 2, y: 2, z: 4, core: 2. Of those that a mesh axis runs over, the one named last changes fastest.
Arguments:
- matrix: float32 [4096, 4096], P('row', 'col'), may hold values from -8 to 48
- pivots: int32 [2, 128], replicated, may hold values from 256 to 4095, as said below
- lower_inverse: float32 [2, 128, 128], replicated, may hold values from -1 to 1, as said below
Outputs:
- factored: float32 [4096, 4096], P('row', 'col')
Inputs may be any that keep to these rules, and one draw needn't show every extreme that they name: pivots[k, j] is the global row that panel k exchanges with global row k * 128 + j; all 256 entries are distinct. Each lower_inverse[k] is unit lower triangular.
All inputs are finite; a program needn't handle non-finite values.
Results may differ from a plain program's by a relative error of at most 0.0001.
Values sent between devices are 32-bit elements; how exact they have to be, the bound alone decides.
A program may use at most 64 MiB of HBM per device.

v0:
```python
import jax
import jax.numpy as jnp
from jax import lax
from jax.sharding import PartitionSpec as P


def spread(value, axis, source):
    kept = jnp.where(lax.axis_index(axis) == source, value, 0).astype(value.dtype)
    return lax.psum(kept, axis)


def exact_dot(left, right):
    return jnp.dot(left, right, precision=lax.Precision.HIGHEST, preferred_element_type=jnp.float32)


def upper_inverse(upper):
    size = upper.shape[0]
    diag_vals = jnp.diagonal(upper)
    scaled = upper / diag_vals[:, None]
    eye_mat = jnp.eye(size, dtype=jnp.float32)
    power = eye_mat - scaled
    result = eye_mat + power
    reach = 2
    while reach < size:
        power = exact_dot(power, power)
        result = exact_dot(result, eye_mat + power)
        reach = reach * 2
    return result / diag_vals[None, :]


def on_device(matrix, pivots, lower_inverse):
    row_count = lax.axis_size("row")
    col_count = lax.axis_size("col")
    row_index = lax.axis_index("row")
    col_index = lax.axis_index("col")
    local_height, local_width = matrix.shape
    block_size = lower_inverse.shape[1]
    row_block = jnp.arange(local_height, dtype=jnp.int32) // block_size * row_count + row_index
    col_spots = jnp.arange(local_width, dtype=jnp.int32)
    col_block = col_spots // block_size * col_count + col_index
    col_inner = col_spots % block_size
    tri_rows = jnp.arange(block_size, dtype=jnp.int32)[:, None]
    height_spots = jnp.arange(local_height, dtype=jnp.int32)

    def owner_table(panel_num):
        pivot_rows = pivots[panel_num]
        pivot_block = pivot_rows // block_size
        is_owned = pivot_block % row_count == row_index
        local_rows = pivot_block // row_count * block_size + pivot_rows % block_size
        return (is_owned[:, None] & (local_rows[:, None] == height_spots[None, :])).astype(
            jnp.float32
        )

    factor_work = matrix
    for panel_num in range(pivots.shape[0]):
        pick_selector = owner_table(panel_num)
        pick_taken_rows = exact_dot(pick_selector, factor_work)
        pick_first_row = panel_num // row_count * block_size
        pick_is_root = panel_num % row_count == row_index
        pick_top_rows = jnp.where(
            pick_is_root, factor_work[pick_first_row : pick_first_row + block_size], 0.0
        )
        swap_taken_rows = pick_taken_rows
        swap_top_rows = pick_top_rows
        swap_taken_rows, swap_top_rows = lax.psum((swap_taken_rows, swap_top_rows), "row")
        place_factor_work = factor_work
        selector = owner_table(panel_num)
        hit_rows = jnp.sum(selector, axis=0) > 0.5
        placed = exact_dot(selector.T, swap_top_rows)
        place_factor_work = jnp.where(hit_rows[:, None], placed, place_factor_work)
        place_first_row = panel_num // row_count * block_size
        place_is_root = panel_num % row_count == row_index
        current = place_factor_work[place_first_row : place_first_row + block_size]
        factor_work = place_factor_work.at[place_first_row : place_first_row + block_size].set(
            jnp.where(place_is_root, swap_taken_rows, current)
        )
        full_factor_work = factor_work
        upper_factor_work = full_factor_work
        first_row = panel_num // row_count * block_size
        upper_block_rows = upper_factor_work[first_row : first_row + block_size]
        upper_is_root = panel_num % row_count == row_index
        product = exact_dot(lower_inverse[panel_num], upper_block_rows)
        diag_part = jnp.where(tri_rows <= col_inner[None, :], product, 0.0)
        upper_formed = spread(
            jnp.where(
                col_block[None, :] > panel_num,
                product,
                jnp.where(col_block[None, :] == panel_num, diag_part, upper_block_rows),
            ),
            "row",
            panel_num % row_count,
        )
        upper_factor_work = upper_factor_work.at[first_row : first_row + block_size].set(
            jnp.where(upper_is_root, upper_formed, upper_block_rows)
        )
        full_factor_work = upper_factor_work
        diag_first_col = panel_num // col_count * block_size
        lower_factor_work = full_factor_work
        lower_first_col = panel_num // col_count * block_size
        panel_cols = lower_factor_work[:, lower_first_col : lower_first_col + block_size]
        inverse_upper = upper_inverse(upper_formed[:, diag_first_col : diag_first_col + block_size])
        solved = exact_dot(panel_cols, inverse_upper)
        is_root = panel_num % col_count == col_index
        is_below = (row_block > panel_num)[:, None] & is_root
        lower_factor_work = lower_factor_work.at[
            :, lower_first_col : lower_first_col + block_size
        ].set(jnp.where(is_below, solved, panel_cols))
        lower_sent_panel = spread(jnp.where(is_below, solved, 0.0), "col", panel_num % col_count)
        full_factor_work = lower_factor_work
        change = exact_dot(lower_sent_panel, upper_formed)
        live = (row_block > panel_num)[:, None] & (col_block > panel_num)[None, :]
        factor_work = full_factor_work.at[:, 0 : 0 + local_width].set(
            jnp.where(live, full_factor_work - change, full_factor_work)
        )
    return factor_work


def solution(mesh):
    return jax.shard_map(
        on_device,
        mesh=mesh,
        in_specs=(P("row", "col"), P(), P()),
        out_specs=P("row", "col"),
        check_vma=False,
    )
```

profile of v0, /device:TPU:0, one launch (start us, length us, event | category | flops | bytes accessed | tf_op | source)
XLA Modules:
  0.0 351.4 jit_solution(4987288827838978806)
XLA Ops:
  6.5 0.9 fusion.56
  7.4 0.8 fusion.54
  8.2 1.7 slice_select_fusion.3
  9.9 3.2 fusion.7
  13.4 48.0 %all-reduce.19.cloned.1.call-done = (f32[128,512]{1,0:T(8,128)}, f32[128,512]{1,0:T(8,128)}) async-done(((f32[128,512]{1,0:T(8,128)}, f32[128,512]{1,0:T(8,128)}), (f32[128,512]{1,0:T(8,128)}, f32[128,512]{1,0:T(8,128)})) %all-reduce.19.cloned.1.call-update) | async-done | bytes 524304 | tf_op jit(solution)/shard_map/psum | solution.py:65
  61.4 2.1 convolution_select_fusion.1
  63.6 1.3 copy-done.3
  64.9 1.2 select_select_fusion.5
  66.1 0.7 compare_reduce_fusion
  66.8 1.6 copy.15
  68.4 40.7 %all-reduce.9.cloned.1.call-done = f32[128,512]{1,0:T(8,128)} async-done(((f32[128,512]{1,0:T(8,128)}), f32[128,512]{1,0:T(8,128)}) %all-reduce.9.cloned.1.call-update) | async-done | bytes 262160 | tf_op jit(solution)/shard_map/psum | solution.py:9
  109.2 0.9 slice.189
  110.1 1.2 gather_fusion
  111.3 1.2 fusion.47
  113.0 1.1 fusion.22
  114.1 0.2 fusion.23
  114.5 0.2 fusion.24
  114.9 0.2 fusion.25
  115.1 0.2 convolution_add_fusion.1
  115.3 0.2 fusion.26
  115.8 1.0 select_dynamic-update-slice_fusion.1
  116.8 0.6 fusion.12
  117.4 1.7 select_select_fusion.3
  119.2 56.2 %all-reduce.11.cloned.1.call-done = f32[1024,128]{1,0:T(8,128)} async-done(((f32[1024,128]{1,0:T(8,128)}), f32[1024,128]{1,0:T(8,128)}) %all-reduce.11.cloned.1.call-update) | async-done | bytes 524304 | tf_op jit(solution)/shard_map/psum | solution.py:9
  175.4 3.7 %subtract_select_fusion.1 = f32[1024,512]{1,0:T(8,128)S(1)} fusion(f32[1024,512]{1,0:T(8,128)} %copy-done, f32[1024,128]{1,0:T(8,128)} %all-reduce.11.cloned.1.call-done, f32[128,512]{1,0:T(8,128)S(1)} %copy-done.4, pred[512]{0:T(512)(128)(4,1)S(1)} %broadcast_compare_fusion.3, pred[1024]{0:T(1024)(128)(4,1)S(1)} %fusion.40), kind=kOutput, calls=%fused_computation.3 | convolution fusion | flops 806879232 | bytes 4982272 | tf_op jit(solution)/shard_map/dot_general | solution.py:13
  179.2 0.7 slice_select_fusion.1
  179.9 1.6 fusion.3
  181.8 44.3 %all-reduce.17.cloned.1.call-done = (f32[128,512]{1,0:T(8,128)}, f32[128,512]{1,0:T(8,128)}) async-done(((f32[128,512]{1,0:T(8,128)}, f32[128,512]{1,0:T(8,128)}), (f32[128,512]{1,0:T(8,128)}, f32[128,512]{1,0:T(8,128)})) %all-reduce.17.cloned.1.call-update) | async-done | bytes 524304 | tf_op jit(solution)/shard_map/psum | solution.py:65
  226.1 2.2 convolution_select_fusion
  228.3 1.3 copy-done.2
  229.6 1.2 select_select_fusion.4
  230.8 0.2 all-reduce.15.cloned.1.call-start
  231.1 1.6 copy.22
  232.7 41.2 %all-reduce.13.cloned.1.call-done = f32[128,512]{1,0:T(8,128)} async-done(((f32[128,512]{1,0:T(8,128)}), f32[128,512]{1,0:T(8,128)}) %all-reduce.13.cloned.1.call-update) | async-done | bytes 262160 | tf_op jit(solution)/shard_map/psum | solution.py:9
  273.9 0.9 slice.193
  274.8 1.2 gather_fusion.1
  276.1 1.2 fusion.48
  277.7 1.1 fusion.27
  278.8 0.2 fusion.28
  279.3 0.2 fusion.29
  279.7 0.2 fusion.30
  280.1 0.2 fusion.31
  280.3 0.2 convolution_divide_fusion
  280.5 1.0 select_dynamic-update-slice_fusion
  281.6 0.6 fusion.10
  282.1 1.7 select_select_fusion.2
  283.9 56.3 %all-reduce.15.cloned.1.call-done = f32[1024,128]{1,0:T(8,128)} async-done(((f32[1024,128]{1,0:T(8,128)}), f32[1024,128]{1,0:T(8,128)}) %all-reduce.15.cloned.1.call-update) | async-done | bytes 524304 | tf_op jit(solution)/shard_map/psum | solution.py:9
  340.2 4.4 %subtract_select_fusion = f32[1024,512]{1,0:T(8,128)} fusion(f32[1024,512]{1,0:T(8,128)S(1)} %get-tuple-element.126, f32[1024,128]{1,0:T(8,128)} %all-reduce.15.cloned.1.call-done, f32[128,512]{1,0:T(8,128)S(1)} %copy-done.5, pred[512]{0:T(512)(128)(4,1)S(1)} %broadcast_compare_fusion.5, pred[1024]{0:T(1024)(128)(4,1)S(1)} %fusion.41), kind=kOutput, calls=%fused_computation.2 | convolution fusion | flops 806879232 | bytes 4982272 | tf_op jit(solution)/shard_map/dot_general | solution.py:13
  (53 shorter events, 2.9 us)
Async XLA Ops:
  6.5 54.9 %copy-start.1 = (f32[1024,512]{1,0:T(8,128)S(1)}, f32[1024,512]{1,0:T(8,128)}, u32[]{:S(2)}) copy-start(f32[1024,512]{1,0:T(8,128)} %param.23) | copy-start | bytes 6291460
  6.5 54.9 %all-reduce.19.cloned.1.call-start = ((), (), s32[]{:S(2)}) async-start(), calls=%async_computation.5 | async-start | bytes 1048576 | tf_op jit(solution)/shard_map/psum | solution.py:65
  13.1 96.1 %all-reduce.9.cloned.1.call-start = ((), (), s32[]{:S(2)}) async-start(), calls=%async_computation | async-start | bytes 524288 | tf_op jit(solution)/shard_map/psum | solution.py:9
  61.4 3.5 copy-start.6
  61.4 3.5 copy-start.8
  63.6 1.3 copy-start.3
  66.1 109.3 %all-reduce.11.cloned.1.call-start = ((), (), s32[]{:S(2)}) async-start(), calls=%async_computation.1 | async-start | bytes 1048576 | tf_op jit(solution)/shard_map/psum | solution.py:9
  109.2 6.6 %copy-start.4 = (f32[128,512]{1,0:T(8,128)S(1)}, f32[128,512]{1,0:T(8,128)}, u32[]{:S(2)}) copy-start(f32[128,512]{1,0:T(8,128)} %all-reduce.9.cloned.1.call-done) | copy-start | bytes 786436
  119.1 56.3 %copy-start = (f32[1024,512]{1,0:T(8,128)}, f32[1024,512]{1,0:T(8,128)S(1)}, u32[]{:S(2)}) copy-start(f32[1024,512]{1,0:T(8,128)S(1)} %get-tuple-element.128) | copy-start | bytes 6291460
  119.1 107.0 %all-reduce.17.cloned.1.call-start = ((), (), s32[]{:S(2)}) async-start(), calls=%async_computation.4 | async-start | bytes 1048576 | tf_op jit(solution)/shard_map/psum | solution.py:65
  181.5 92.4 %all-reduce.13.cloned.1.call-start = ((), (), s32[]{:S(2)}) async-start(), calls=%async_computation.2 | async-start | bytes 524288 | tf_op jit(solution)/shard_map/psum | solution.py:9
  226.1 3.5 copy-start.7
  228.3 1.3 copy-start.2
  230.8 109.4 %all-reduce.15.cloned.1.call-start = ((), (), s32[]{:S(2)}) async-start(), calls=%async_computation.3 | async-start | bytes 1048576 | tf_op jit(solution)/shard_map/psum | solution.py:9
  273.9 6.6 %copy-start.5 = (f32[128,512]{1,0:T(8,128)S(1)}, f32[128,512]{1,0:T(8,128)}, u32[]{:S(2)}) copy-start(f32[128,512]{1,0:T(8,128)} %all-reduce.13.cloned.1.call-done) | copy-start | bytes 786436
Sparse Core Ops, SparseCore 0:
  13.2 48.1 all-reduce.18
  66.2 42.9 all-reduce.8
  119.3 56.1 all-reduce.10
  181.6 44.4 all-reduce.16
  230.9 42.9 all-reduce.12
  284.0 56.1 all-reduce.14
where the time goes:
time: 352 us; the launch traced here: 351 us
  waiting for transfers between devices  287 us (82%)
  matrix products  29.4 us (8%)
  between operations  13.9 us (4%)
  other arithmetic  10.7 us (3%)
  local copies, waits for them, and re-layouts  10.2 us (3%)
    psum x4, waiting for transfers between devices, spread(): return lax.psum(kept, axis)  194 us
    psum x2, waiting for transfers between devices, on_device(): lax.psum((swap_taken_rows, swap_top_rows), 'row')  92.4 us
    dot_general x34, matrix products, exact_dot(): jnp.dot(left, right, precision=lax.Precision.HIGHEST, preferred_element_t...  29.4 us
  transfers between devices with their start and end apart: 6, of which 6 were waited for; matrix products, arithmetic and copies ran while one was open for 1% of the time, Pallas kernels for 0%

commit v1 on v0

--- a/solution.py
+++ b/solution.py
@@ -6,7 +6,7 @@
 
 def spread(value, axis, source):
     kept = jnp.where(lax.axis_index(axis) == source, value, 0).astype(value.dtype)
-    return lax.psum(kept, axis)
+    return lax.all_gather(kept, axis).sum(axis=0)
 
 
 def exact_dot(left, right):

time: 352 us -> 302 us (0.86)
  waiting for transfers between devices: 287 us -> 236 us
  other arithmetic: 10.7 us -> 18.5 us
  matrix products: 29.4 us -> 24.6 us
    psum x4 -> x0, waiting for transfers between devices: 194 us -> none  [spread(): return lax.psum(kept, axis)]
    all_gather x0 -> x4, waiting for transfers between devices: none -> 144 us  [spread(): return lax.all_gather(kept, axis).sum(axis=0)]
    reduce_sum x0 -> x4, other arithmetic: none -> 7.58 us  [spread(): return lax.all_gather(kept, axis).sum(axis=0)]
    dot_general x34, matrix products: 29.4 us -> 24.6 us  [exact_dot(): jnp.dot(left, right, precision=lax.Precision.HIGHEST, preferred_element_t...]
where the time goes in v1:
time: 302 us
  waiting for transfers between devices  236 us (78%)
  matrix products  24.6 us (8%)
  other arithmetic  18.5 us (6%)
  between operations  13.9 us (5%)
  local copies, waits for them, and re-layouts  8.34 us (3%)
    all_gather x4, waiting for transfers between devices, spread(): return lax.all_gather(kept, axis).sum(axis=0)  144 us
    psum x2, waiting for transfers between devices, on_device(): lax.psum((swap_taken_rows, swap_top_rows), 'row')  92.2 us
    dot_general x34, matrix products, exact_dot(): jnp.dot(left, right, precision=lax.Precision.HIGHEST, preferred_element_t...  24.6 us
    reduce_sum x4, other arithmetic, spread(): return lax.all_gather(kept, axis).sum(axis=0)  7.58 us
  transfers between devices with their start and end apart: 6, of which 6 were waited for; matrix products, arithmetic and copies ran while one was open for 1% of the time, Pallas kernels for 0%

profile of v1, /device:TPU:0, one launch (start us, length us, event | category | flops | bytes accessed | tf_op | source)
XLA Modules:
  0.0 301.7 jit_solution(6749872421816810640)
XLA Ops:
  6.5 0.9 fusion.56
  7.4 0.8 fusion.54
  8.2 1.7 slice_select_fusion.3
  9.9 3.2 %fusion.7 = f32[128,512]{1,0:T(8,128)} fusion(f32[1024,512]{1,0:T(8,128)} %param.23, s32[128]{0:T(128)S(1)} %get-tuple-element.130, pred[128]{0:T(512)(128)(4,1)S(1)} %get-tuple-element.131), kind=kOutput, calls=%fused_computation.25 | convolution fusion | flops 805568512 | bytes 2359936 | tf_op jit(solution)/shard_map/dot_general | solution.py:13
  13.3 48.1 %all-reduce.7.cloned.1.call-done = (f32[128,512]{1,0:T(8,128)}, f32[128,512]{1,0:T(8,128)}) async-done(((f32[128,512]{1,0:T(8,128)}, f32[128,512]{1,0:T(8,128)}), (f32[128,512]{1,0:T(8,128)}, f32[128,512]{1,0:T(8,128)})) %all-reduce.7.cloned.1.call-update) | async-done | bytes 524304 | tf_op jit(solution)/shard_map/psum | solution.py:65
  61.4 2.1 convolution_select_fusion.1
  63.6 1.3 copy-done.3
  64.9 1.2 select_select_fusion.5
  66.1 0.7 compare_reduce_fusion
  66.8 1.6 copy.14
  68.5 24.3 %all-gather.9.cloned.1.call-done = f32[512,512]{1,0:T(8,128)} async-done(((f32[128,512]{1,0:T(8,128)}), f32[512,512]{1,0:T(8,128)}) %all-gather.9.cloned.1.call-update) | async-done | bytes 1048592 | tf_op jit(solution)/shard_map/all_gather | solution.py:9
  92.8 1.3 reduce_sum.56
  94.2 1.2 gather_fusion
  95.4 0.3 fusion.47
  95.7 0.3 fusion.22
  96.2 1.0 select_dynamic-update-slice_fusion.1
  97.4 0.2 fusion.23
  97.9 0.2 fusion.24
  98.3 0.2 fusion.25
  98.7 0.2 fusion.26
  99.1 0.6 fusion.12
  99.7 1.8 select_select_fusion.3
  101.6 47.2 %all-gather.11.cloned.1.call-done = f32[8192,128]{1,0:T(8,128)} async-done(((f32[1024,128]{1,0:T(8,128)}), f32[8192,128]{1,0:T(8,128)}) %all-gather.11.cloned.1.call-update) | async-done | bytes 4194320 | tf_op jit(solution)/shard_map/all_gather | solution.py:9
  148.8 2.5 reduce_sum.57
  151.3 3.6 %subtract_select_fusion.1 = f32[1024,512]{1,0:T(8,128)S(1)} fusion(f32[1024,512]{1,0:T(8,128)} %copy-done, f32[1024,128]{1,0:T(8,128)S(1)} %reduce_sum.57, f32[128,512]{1,0:T(8,128)S(1)} %reduce_sum.56, pred[512]{0:T(512)(128)(4,1)S(1)} %get-tuple-element.134, pred[1024]{0:T(1024)(128)(4,1)S(1)} %fusion.40), kind=kOutput, calls=%fused_computation.3 | convolution fusion | flops 806879232 | bytes 4982272 | tf_op jit(solution)/shard_map/dot_general | solution.py:13
  154.9 0.7 slice_select_fusion.1
  155.6 1.6 fusion.3
  157.5 44.1 %all-reduce.5.cloned.1.call-done = (f32[128,512]{1,0:T(8,128)}, f32[128,512]{1,0:T(8,128)}) async-done(((f32[128,512]{1,0:T(8,128)}, f32[128,512]{1,0:T(8,128)}), (f32[128,512]{1,0:T(8,128)}, f32[128,512]{1,0:T(8,128)})) %all-reduce.5.cloned.1.call-update) | async-done | bytes 524304 | tf_op jit(solution)/shard_map/psum | solution.py:65
  201.6 2.2 convolution_select_fusion
  203.8 1.3 copy-done.2
  205.1 1.2 select_select_fusion.4
  206.3 0.2 all-gather.15.cloned.1.call-start
  206.5 1.6 copy.19
  208.2 24.9 %all-gather.13.cloned.1.call-done = f32[512,512]{1,0:T(8,128)} async-done(((f32[128,512]{1,0:T(8,128)}), f32[512,512]{1,0:T(8,128)}) %all-gather.13.cloned.1.call-update) | async-done | bytes 1048592 | tf_op jit(solution)/shard_map/all_gather | solution.py:9
  233.1 1.3 reduce_sum.58
  234.4 1.2 gather_fusion.1
  235.7 0.3 fusion.48
  236.0 0.3 fusion.27
  236.4 1.0 select_dynamic-update-slice_fusion
  237.7 0.2 fusion.28
  238.1 0.2 fusion.29
  238.5 0.2 fusion.30
  239.0 0.2 fusion.31
  239.4 0.6 fusion.10
  240.0 1.8 select_select_fusion.2
  241.8 47.3 %all-gather.15.cloned.1.call-done = f32[8192,128]{1,0:T(8,128)} async-done(((f32[1024,128]{1,0:T(8,128)}), f32[8192,128]{1,0:T(8,128)}) %all-gather.15.cloned.1.call-update) | async-done | bytes 4194320 | tf_op jit(solution)/shard_map/all_gather | solution.py:9
  289.1 2.5 reduce_sum.59
  291.5 3.3 %subtract_select_fusion = f32[1024,512]{1,0:T(8,128)} fusion(f32[1024,512]{1,0:T(8,128)S(1)} %get-tuple-element.126, f32[1024,128]{1,0:T(8,128)S(1)} %reduce_sum.59, f32[128,512]{1,0:T(8,128)S(1)} %reduce_sum.58, pred[512]{0:T(512)(128)(4,1)S(1)} %broadcast_compare_fusion.5, pred[1024]{0:T(1024)(128)(4,1)S(1)} %fusion.41), kind=kOutput, calls=%fused_computation.2 | convolution fusion | flops 806879232 | bytes 4982272 | tf_op jit(solution)/shard_map/dot_general | solution.py:13
  (52 shorter events, 3.3 us)
Async XLA Ops:
  6.5 54.9 %copy-start.1 = (f32[1024,512]{1,0:T(8,128)S(1)}, f32[1024,512]{1,0:T(8,128)}, u32[]{:S(2)}) copy-start(f32[1024,512]{1,0:T(8,128)} %param.23) | copy-start | bytes 6291460
  6.5 54.9 %all-reduce.7.cloned.1.call-start = ((), (), s32[]{:S(2)}) async-start(), calls=%async_computation.5 | async-start | bytes 1048576 | tf_op jit(solution)/shard_map/psum | solution.py:65
  13.1 79.8 %all-gather.9.cloned.1.call-start = ((), (), s32[]{:S(2)}) async-start(), calls=%async_computation | async-start | bytes 1310720 | tf_op jit(solution)/shard_map/all_gather | solution.py:9
  61.4 3.5 %copy-start.4 = (f32[128,512]{1,0:T(8,128)S(1)}, f32[128,512]{1,0:T(8,128)}, u32[]{:S(2)}) copy-start(f32[128,512]{1,0:T(8,128)} %get-tuple-element.120) | copy-start | bytes 786436
  61.4 3.5 %copy-start.6 = (f32[2,128,128]{2,1,0:T(8,128)S(1)}, f32[2,128,128]{2,1,0:T(8,128)}, u32[]{:S(2)}) copy-start(f32[2,128,128]{2,1,0:T(8,128)} %param.25) | copy-start | bytes 393220
  63.5 1.3 copy-start.3
  66.1 82.8 %all-gather.11.cloned.1.call-start = ((), (), s32[]{:S(2)}) async-start(), calls=%async_computation.1 | async-start | bytes 4718592 | tf_op jit(solution)/shard_map/all_gather | solution.py:9
  101.5 49.8 %copy-start = (f32[1024,512]{1,0:T(8,128)}, f32[1024,512]{1,0:T(8,128)S(1)}, u32[]{:S(2)}) copy-start(f32[1024,512]{1,0:T(8,128)S(1)} %get-tuple-element.128) | copy-start | bytes 6291460
  101.5 100.1 %all-reduce.5.cloned.1.call-start = ((), (), s32[]{:S(2)}) async-start(), calls=%async_computation.4 | async-start | bytes 1048576 | tf_op jit(solution)/shard_map/psum | solution.py:65
  157.2 75.8 %all-gather.13.cloned.1.call-start = ((), (), s32[]{:S(2)}) async-start(), calls=%async_computation.2 | async-start | bytes 1310720 | tf_op jit(solution)/shard_map/all_gather | solution.py:9
  201.6 3.5 %copy-start.5 = (f32[128,512]{1,0:T(8,128)S(1)}, f32[128,512]{1,0:T(8,128)}, u32[]{:S(2)}) copy-start(f32[128,512]{1,0:T(8,128)} %get-tuple-element.118) | copy-start | bytes 786436
  203.8 1.3 copy-start.2
  206.3 82.8 %all-gather.15.cloned.1.call-start = ((), (), s32[]{:S(2)}) async-start(), calls=%async_computation.3 | async-start | bytes 4718592 | tf_op jit(solution)/shard_map/all_gather | solution.py:9
Sparse Core Ops, SparseCore 0:
  13.2 48.1 all-reduce.6
  66.2 26.6 all-gather.8
  101.7 47.1 all-gather.10
  157.4 44.1 all-reduce.4
  206.4 26.6 all-gather.12
  241.9 47.1 all-gather.14
